TPU v7x, 256 devices: a whole 4x4x8 slice. The times are simulated.
256 devices in a mesh: row: 8 (over z), col: 16 (over x, y), rep: 2 (over core).
Axes of the slice: x: 4, y: 4, z: 8, core: 2. Of those that a mesh axis runs over, the one named last changes fastest.
Arguments:
- density: bfloat16 [6144, 6144], P('row', 'col')
- pattern: int32 [48, 48], replicated, may hold values from 0 to 1, as said below
- keep: int32 [2, 48, 48], replicated, may hold values from 0 to 1, as said below
Outputs:
- purified: bfloat16 [6144, 6144], P('row', 'col')
Inputs may be any that keep to these rules, and one draw needn't show every extreme that they name: density is symmetric. pattern is symmetric, 0 or 1, with ones on the diagonal. Each keep[s] is symmetric, 0 or 1, with ones on the diagonal.
All inputs are finite; a program needn't handle non-finite values.
Results may differ from a plain program's by a relative error of at most 0.0057.
Values may be sent and summed in bfloat16 or wider, within the bound.
A program may use at most 64 MiB of HBM per device.

v0:
```python
import jax
import jax.numpy as jnp
from jax import lax
from jax.sharding import PartitionSpec as P

BS = 128


def expand(mask):
    return jnp.repeat(jnp.repeat(mask, BS, axis=0), BS, axis=1) > 0


def shards(density, pattern, keep):
    rows_tile, cols_tile = density.shape
    row_blocks = rows_tile // BS
    col_blocks = cols_tile // BS
    row_index = lax.axis_index("row")
    col_index = lax.axis_index("col")
    rep_index = lax.axis_index("rep")
    half = cols_tile // 2

    def local_mask(mask):
        window = lax.dynamic_slice(
            mask, (row_index * row_blocks, col_index * col_blocks), (row_blocks, col_blocks)
        )
        return expand(window)

    current = jnp.where(local_mask(pattern), density, jnp.zeros_like(density))
    for step in range(2):
        left_half = lax.dynamic_slice_in_dim(current, rep_index * half, half, 1)
        stacked = current.reshape(rows_tile // cols_tile, 2, half, cols_tile)
        right_half = lax.dynamic_index_in_dim(stacked, rep_index, 1, keepdims=False)
        right_half = right_half.reshape(rows_tile // 2, cols_tile)
        column_rows = lax.all_gather(right_half, "row", axis=0, tiled=True)
        partial_sum = jnp.dot(
            lax.all_gather(left_half, "col", axis=1, tiled=True),
            column_rows,
            preferred_element_type=jnp.float32,
        )
        kept = local_mask(keep[step])
        square = lax.psum(partial_sum, "rep")
        before = current.astype(jnp.float32)
        updated = 2.0 * before - square if step == 1 else square
        updated = jnp.where(kept, updated, jnp.zeros_like(updated))
        current = updated.astype(jnp.bfloat16)
    return current


def solution(mesh):
    in_specs = (P("row", "col"), P(), P())
    out_specs = P("row", "col")
    return jax.shard_map(shards, mesh=mesh, in_specs=in_specs, out_specs=out_specs, check_vma=False)
```

profile of v0, /device:TPU:1, one launch (start us, length us, event | category | flops | bytes accessed | tf_op | source)
XLA Modules:
  0.0 277.1 jit_solution(11129041823438781943)
XLA Ops:
  6.5 0.0 all-gather.7.cloned.1.call-start
  6.5 0.8 dynamic-slice_compare_fusion
  7.3 0.1 copy.23
  7.4 0.1 broadcast_bitcast_fusion
  7.5 1.3 copy.24
  8.8 0.0 copy-start
  8.8 0.1 bitcast_select_fusion
  8.9 0.3 copy.25
  9.2 0.8 constant_dynamic-slice_fusion.1
  10.0 0.0 all-gather.7.cloned.1.call-update
  10.0 0.0 all-gather.5.cloned.1.call-start
  10.0 0.7 constant_dynamic-slice_fusion.2
  10.8 0.0 all-gather.5.cloned.1.call-update
  10.8 0.0 all-gather.11.cloned.1.call-start
  10.8 0.0 copy-done
  10.9 0.1 dynamic-slice_compare_fusion.1
  11.0 0.1 copy.22
  11.1 0.1 broadcast_bitcast_fusion.1
  11.2 0.1 broadcast_in_dim.24
  11.2 0.5 copy.26
  11.7 40.9 %all-gather.7.cloned.1.call-done = bf16[3072,384]{1,0:T(8,128)(2,1)} async-done(((bf16[384,384]{1,0:T(8,128)(2,1)}), bf16[3072,384]{1,0:T(8,128)(2,1)}) %all-gather.7.cloned.1.call-update) | async-done | bytes 2359312 | tf_op jit(solution)/shard_map/all_gather | solution.py:34
  52.6 63.2 %all-gather.5.cloned.1.call-done = bf16[768,3072]{0,1:T(8,128)(2,1)} async-done(((bf16[768,192]{0,1:T(8,128)(2,1)}), bf16[768,3072]{0,1:T(8,128)(2,1)}) %all-gather.5.cloned.1.call-update) | async-done | bytes 4718608 | tf_op jit(solution)/shard_map/all_gather | solution.py:36
  115.8 5.2 %fusion.1 = f32[768,384]{1,0:T(8,128)S(1)} fusion(bf16[768,3072]{0,1:T(8,128)(2,1)} %all-gather.5.cloned.1.call-done, bf16[3072,384]{1,0:T(8,128)(2,1)} %all-gather.7.cloned.1.call-done), kind=kOutput, calls=%fused_computation.17 | convolution fusion | flops 1811939328 | bytes 8257536 | tf_op jit(solution)/shard_map/dot_general | solution.py:35
  121.0 7.1 %all-reduce.4 = bf16[768,384]{1,0:T(8,128)(2,1)S(1)} all-reduce(f32[768,384]{1,0:T(8,128)S(1)} %fusion.1), channel_id=1, replica_groups=mesh['row'=8,'col'=16,'rep'=2] {'rep'}, use_global_device_ids=true, to_apply=%region_0.1 | all-reduce | flops 294912 | bytes 1769472 | tf_op jit(solution)/shard_map/psum | solution.py:41
  128.1 0.2 select_convert_fusion.1
  128.3 0.8 constant_dynamic-slice_fusion.3
  129.1 0.0 all-gather.11.cloned.1.call-update
  129.1 0.0 all-gather.9.cloned.1.call-start
  129.1 0.2 constant_dynamic-slice_fusion
  129.3 0.9 copy.27
  130.2 0.0 all-gather.9.cloned.1.call-update
  130.2 0.0 all-reduce.3.cloned.1.call-start
  130.3 36.8 %all-gather.11.cloned.1.call-done = bf16[3072,384]{1,0:T(8,128)(2,1)} async-done(((bf16[384,384]{1,0:T(8,128)(2,1)}), bf16[3072,384]{1,0:T(8,128)(2,1)}) %all-gather.11.cloned.1.call-update) | async-done | bytes 2359312 | tf_op jit(solution)/shard_map/all_gather | solution.py:34
  167.1 63.1 %all-gather.9.cloned.1.call-done = bf16[768,3072]{0,1:T(8,128)(2,1)} async-done(((bf16[768,192]{0,1:T(8,128)(2,1)}), bf16[768,3072]{0,1:T(8,128)(2,1)}) %all-gather.9.cloned.1.call-update) | async-done | bytes 4718608 | tf_op jit(solution)/shard_map/all_gather | solution.py:36
  230.2 6.8 %fusion.2 = f32[768,384]{1,0:T(8,128)} fusion(bf16[768,3072]{0,1:T(8,128)(2,1)} %all-gather.9.cloned.1.call-done, bf16[3072,384]{1,0:T(8,128)(2,1)} %all-gather.11.cloned.1.call-done), kind=kOutput, calls=%fused_computation.18 | convolution fusion | flops 1811939328 | bytes 8257536 | tf_op jit(solution)/shard_map/dot_general | solution.py:35
  236.9 0.0 all-reduce.3.cloned.1.call-update
  237.0 0.1 copy.21
  237.1 0.1 broadcast_bitcast_fusion.2
  237.2 0.1 broadcast_in_dim.22
  237.2 0.5 copy.28
  237.7 30.5 %all-reduce.3.cloned.1.call-done = f32[768,384]{1,0:T(8,128)} async-done(((f32[768,384]{1,0:T(8,128)}), f32[768,384]{1,0:T(8,128)}) %all-reduce.3.cloned.1.call-update) | async-done | bytes 1179664 | tf_op jit(solution)/shard_map/psum | solution.py:41
  268.2 2.3 select_convert_fusion
  (4 shorter events, 0.0 us)
Async XLA Ops:
  6.5 46.0 %all-gather.7.cloned.1.call-start = ((), (), s32[]{:S(2)}) async-start(), calls=%async_computation.1 | async-start | bytes 2654208 | tf_op jit(solution)/shard_map/all_gather | solution.py:34
  8.8 2.0 copy-start
  10.0 105.8 %all-gather.5.cloned.1.call-start = ((), (), s32[]{:S(2)}) async-start(), calls=%async_computation | async-start | bytes 5013504 | tf_op jit(solution)/shard_map/all_gather | solution.py:36
  10.8 156.3 %all-gather.11.cloned.1.call-start = ((), (), s32[]{:S(2)}) async-start(), calls=%async_computation.3 | async-start | bytes 2654208 | tf_op jit(solution)/shard_map/all_gather | solution.py:34
  129.1 101.1 %all-gather.9.cloned.1.call-start = ((), (), s32[]{:S(2)}) async-start(), calls=%async_computation.2 | async-start | bytes 5013504 | tf_op jit(solution)/shard_map/all_gather | solution.py:36
  130.2 138.0 %all-reduce.3.cloned.1.call-start = ((), (), s32[]{:S(2)}) async-start(), calls=%async_computation.4 | async-start | bytes 2359296 | tf_op jit(solution)/shard_map/psum | solution.py:41
Sparse Core Ops, SparseCore 0:
  10.1 42.4 all-gather.6
  55.0 60.7 all-gather.4
  129.2 37.8 all-gather.10
  169.4 60.7 all-gather.8
  237.1 31.0 all-reduce.2
where the time goes:
time: 277 us
  waiting for transfers between devices  235 us (85%)
  between operations  13.2 us (5%)
  matrix products  12 us (4%)
  blocking collectives  7.08 us (3%)
  local copies, waits for them, and re-layouts  6.62 us (2%)
  other arithmetic  3.44 us (1%)
    all_gather x2, waiting for transfers between devices, shards(): lax.all_gather(left_half, 'col', axis=1, tiled=True)  126 us
    all_gather x2, waiting for transfers between devices, shards(): column_rows = lax.all_gather(right_half, 'row', axis=0, tiled=True)  77.7 us
    psum x1, waiting for transfers between devices, shards(): square = lax.psum(partial_sum, 'rep')  30.5 us
    dot_general x2, matrix products, shards(): jnp.dot(lax.all_gather(left_half, 'col', axis=1, tiled=True), column_rows...  12 us
    psum x1, blocking collectives, shards(): square = lax.psum(partial_sum, 'rep')  7.08 us
  transfers between devices with their start and end apart: 5, of which 5 were waited for; matrix products, arithmetic and copies ran while one was open for 1% of the time, Pallas kernels for 0%

commit v1 on v0

v1 whole, which is shorter than its diff:
```python
import functools

import jax
import jax.numpy as jnp
from jax import lax
from jax.experimental import pallas as pl
from jax.experimental.pallas import tpu as pltpu
from jax.sharding import PartitionSpec as P

BS = 128
NX, NY, NZ = 4, 4, 8
H = 384
CH = 96
MESH = pl.DeviceIdType.MESH

ORDER = [
    (0, 0), (1, 0), (3, 0), (0, 1), (0, 3), (3, 3), (3, 1), (1, 3),
    (1, 1), (2, 0), (0, 2), (3, 2), (2, 3), (1, 2), (2, 1), (2, 2),
]
SLOT = {place: i for i, place in enumerate(ORDER)}


def queues():
    along, back = [], []
    for queue, behind, keep in ((along, 3, 0), (back, 1, 1)):
        pair = (0, 1) if keep == 0 else (1, 0)
        first = [((0, 0), c) for c in pair]
        own = [((0, 0), 2 + c) for c in pair]
        queue += first + own
        queue += [((behind, 0), keep)]
        for other in (3, 1):
            queue += [((0, other), 2 + c) for c in pair]
        queue += [((behind, 0), 2 + keep)]
        queue += [((0, 2), 2 + c) for c in pair]
        queue += [((behind, other), 2 + keep) for other in (3, 1, 2)]

    def swapped(queue):
        return [((dy, dx), (c + 2) % 4) for (dx, dy), c in queue]

    up = [(0, c) for c in range(4)] + [(7, c) for c in range(4)]
    up += [(6, c) for c in range(4)] + [(5, c) for c in (0, 1)]
    down = [(0, c) for c in (3, 2, 1, 0)] + [(1, c) for c in (3, 2, 1, 0)]
    down += [(2, c) for c in (3, 2, 1, 0)] + [(3, c) for c in (3, 2)]
    return [along, back, swapped(along), swapped(back), up, down]


QUEUES = queues()

STAGES = [
    (9, 5, 1, 0),
    (11, 6, 1, 1),
    (13, 9, 2, 1),
    (15, 11, 2, 2),
    (16, 11, 3, 2),
    (17, 13, 3, 3),
    (18, 15, 4, 3),
    (19, 16, 4, 4),
]


def kernel(pattern, keep, density, out, a0, a1, b0, b1, acc, own,
           recv_a, recv_b, recv_c, send, misc):
    z = lax.axis_index("row")
    col = lax.axis_index("col")
    r = lax.axis_index("rep")
    x, y = col // NY, col % NY

    def at(dx, dy, dz):
        return ((z + dz) % NZ, ((x + dx) % NX) * NY + (y + dy) % NY, r)

    targets = [at(1, 0, 0), at(3, 0, 0), at(0, 1, 0), at(0, 3, 0), at(0, 0, 1), at(0, 0, 7)]
    other_core = (z, col, 1 - r)
    half = pl.ds(pl.multiple_of(r * H, H), H)

    load = pltpu.make_async_copy(density.at[half], own, misc.at[0])
    load.start()
    barrier = pltpu.get_barrier_semaphore()
    for target in targets + [other_core]:
        pl.semaphore_signal(barrier, inc=1, device_id=target, device_id_type=MESH)
    load.wait()

    def masked_store(mask, value, stores):
        for i in range(3):
            rows = slice(i * BS, (i + 1) * BS)
            for j in range(3):
                cols = slice(j * BS, (j + 1) * BS)
                kept = mask(z * 6 + r * 3 + i, col * 3 + j) > 0
                block = value(rows, cols)
                block = jnp.where(kept, block, jnp.zeros_like(block)).astype(jnp.bfloat16)
                for store in stores:
                    store[rows, cols] = block

    masked_store(
        lambda i, j: pattern[i, j], lambda rows, cols: own[rows, cols], [a0.at[0], b0.at[0, r]]
    )
    pl.semaphore_wait(barrier, 7)

    for step, (a, b) in enumerate(((a0, b0), (a1, b1))):
        waited = set()

        def dst_place(direction, place):
            if direction < 4:
                dx, dy = place
                shift = ((3, 0), (1, 0), (0, 3), (0, 1))[direction]
                return ((dx + shift[0]) % 4, (dy + shift[1]) % 4)
            return (place + (7, 1)[direction - 4]) % 8

        def piece_a(place, chunk):
            return a.at[SLOT[place], pl.ds(chunk * CH, CH)]

        def piece_b(place, chunk):
            return b.at[place, r, pl.ds(chunk * CH, CH)]

        def ensure_a(place, chunk):
            if place == (0, 0) or ("a", place, chunk) in waited:
                return
            waited.add(("a", place, chunk))
            ref = piece_a(place, chunk)
            pltpu.make_async_copy(ref, ref, recv_a.at[step, SLOT[place], chunk]).wait()

        def ensure_b(place, chunk):
            if place == 0 or ("b", place, chunk) in waited:
                return
            waited.add(("b", place, chunk))
            ref = piece_b(place, chunk)
            pltpu.make_async_copy(ref, ref, recv_b.at[step, place, chunk]).wait()

        def ensure_c(place):
            if ("c", place) in waited:
                return
            waited.add(("c", place))
            ref = b.at[place, 1 - r]
            pltpu.make_async_copy(ref, ref, recv_c.at[step, place]).wait()

        def share(place):
            if ("s", place) in waited:
                return
            waited.add(("s", place))
            pltpu.make_async_remote_copy(
                src_ref=b.at[place, r], dst_ref=b.at[place, r],
                send_sem=send.at[step, 6], recv_sem=recv_c.at[step, place],
                device_id=other_core, device_id_type=MESH,
            ).start()

        def issue(k):
            for direction, queue in enumerate(QUEUES):
                if k >= len(queue):
                    continue
                place, chunk = queue[k]
                if direction < 4:
                    ensure_a(place, chunk)
                    src = piece_a(place, chunk)
                    there = dst_place(direction, place)
                    dst = piece_a(there, chunk)
                    sem = recv_a.at[step, SLOT[there], chunk]
                else:
                    ensure_b(place, chunk)
                    src = piece_b(place, chunk)
                    there = dst_place(direction, place)
                    dst = piece_b(there, chunk)
                    sem = recv_b.at[step, there, chunk]
                pltpu.make_async_remote_copy(
                    src_ref=src, dst_ref=dst, send_sem=send.at[step, direction], recv_sem=sem,
                    device_id=targets[direction], device_id_type=MESH,
                ).start()

        def products(tiles, mine, shared, before):
            tiles0, mine0, shared0 = before

            def body(i, carry):
                dx, dy = jnp.int32(0), jnp.int32(0)
                for j, place in enumerate(ORDER[:tiles]):
                    if place != (0, 0):
                        dx = jnp.where(i == j, place[0], dx)
                        dy = jnp.where(i == j, place[1], dy)
                panel = ((x + dx) % NX) * NY + (y + dy) % NY
                rp = panel % 2
                dz = (panel // 2 + NZ - z) % NZ
                far = jnp.where(dz > 4, NZ - dz, dz)
                reach = jnp.where(rp == r, mine, shared)
                reach0 = jnp.where(rp == r, mine0, shared0)
                ready = jnp.where(far <= reach, 1, 0)
                done = jnp.where((i < tiles0) & (far <= reach0), 1, 0)

                @pl.when(ready > done)
                def _():
                    acc[...] += jnp.dot(a[i], b[dz, rp], preferred_element_type=jnp.float32)

                return carry

            lax.fori_loop(0, tiles, body, 0)

        for k in range(4):
            issue(k)
        share(0)
        acc[...] = jnp.zeros_like(acc)

        stages = list(STAGES)
        before = (0, -1, -1)
        for k in range(4, 20):
            if k < 15:
                issue(k)
            for near in range(1, 5):
                for place in {near, NZ - near}:
                    if all(("b", place, c) in waited for c in range(4)):
                        share(place)
            if stages and stages[0][0] == k + 1 or k >= 15 and stages:
                _, tiles, mine, shared = stages.pop(0)
                for place in ORDER[:tiles]:
                    for c in range(4):
                        ensure_a(place, c)
                for near in range(1, mine + 1):
                    for place in sorted({near, NZ - near}):
                        for c in range(4):
                            ensure_b(place, c)
                        share(place)
                for near in range(0, shared + 1):
                    for place in sorted({near, (NZ - near) % NZ}):
                        ensure_c(place)
                if not stages:
                    for direction, queue in enumerate(QUEUES):
                        n = len(queue)
                        ref = a.at[pl.ds(0, n), pl.ds(0, CH)]
                        pltpu.make_async_copy(ref, ref, send.at[step, direction]).wait()
                    ref = b.at[:, 0]
                    pltpu.make_async_copy(ref, ref, send.at[step, 6]).wait()
                products(tiles, mine, shared, before)
                before = (tiles, mine, shared)

        if step == 0:
            masked_store(
                lambda i, j: keep[0, i, j], lambda rows, cols: acc[rows, cols],
                [a1.at[0], b1.at[0, r]],
            )
        else:
            masked_store(
                lambda i, j: keep[1, i, j],
                lambda rows, cols: 2.0 * a[0, rows, cols].astype(jnp.float32) - acc[rows, cols],
                [own],
            )
    remote = pltpu.make_async_remote_copy(
        src_ref=own, dst_ref=out.at[half], send_sem=misc.at[1], recv_sem=misc.at[2],
        device_id=other_core, device_id_type=MESH,
    )
    remote.start()
    local = pltpu.make_async_copy(own, out.at[half], misc.at[0])
    local.start()
    local.wait()
    remote.wait()


def shards(density, pattern, keep):
    smem = pl.BlockSpec(memory_space=pltpu.SMEM)
    hbm = pl.BlockSpec(memory_space=pl.ANY)
    bf16 = jnp.bfloat16
    return pl.pallas_call(
        kernel,
        out_shape=jax.ShapeDtypeStruct(density.shape, bf16),
        in_specs=[smem, smem, hbm],
        out_specs=hbm,
        scratch_shapes=[
            pltpu.VMEM((16, H, H), bf16),
            pltpu.VMEM((16, H, H), bf16),
            pltpu.VMEM((NZ, 2, H, H), bf16),
            pltpu.VMEM((NZ, 2, H, H), bf16),
            pltpu.VMEM((H, H), jnp.float32),
            pltpu.VMEM((H, H), bf16),
            pltpu.SemaphoreType.DMA((2, 16, 4)),
            pltpu.SemaphoreType.DMA((2, NZ, 4)),
            pltpu.SemaphoreType.DMA((2, NZ)),
            pltpu.SemaphoreType.DMA((2, 7)),
            pltpu.SemaphoreType.DMA((3,)),
        ],
        name="purify",
        cost_estimate=pl.CostEstimate(flops=2 * 2 * H * H * 6144, bytes_accessed=2 * 768 * H * 2, transcendentals=0),
        compiler_params=pltpu.CompilerParams(
            collective_id=0, has_side_effects=True, vmem_limit_bytes=48 * 2**20
        ),
    )(pattern, keep, density)


def solution(mesh):
    in_specs = (P("row", "col"), P(), P())
    out_specs = P("row", "col")
    return jax.shard_map(shards, mesh=mesh, in_specs=in_specs, out_specs=out_specs, check_vma=False)
```

time: 277 us -> 74.7 us (0.27)
  waiting for transfers between devices: 235 us -> 0 us
  Pallas kernels: 0 us -> 71 us
  between operations: 13.2 us -> 0.01 us
  matrix products: 12 us -> 0 us
  blocking collectives: 7.08 us -> 0 us
  other arithmetic: 3.44 us -> 0 us
  local copies, waits for them, and re-layouts: 6.62 us -> 3.42 us
    all_gather x4 -> x0, waiting for transfers between devices: 204 us -> none  [the longest x2 126 us: shards(): lax.all_gather(left_half, 'col', axis=1, tiled=True)]
    pallas_call x0 -> x1, Pallas kernels: none -> 71 us  [shards(): pl.pallas_call(kernel, out_shape=jax.ShapeDtypeStruct(density.shape, bf16...]
    psum x1 -> x0, waiting for transfers between devices: 30.5 us -> none  [shards(): square = lax.psum(partial_sum, 'rep')]
    dot_general x2 -> x0, matrix products: 12 us -> none  [shards(): jnp.dot(lax.all_gather(left_half, 'col', axis=1, tiled=True), column_rows...]
    psum x1 -> x0, blocking collectives: 7.08 us -> none  [shards(): square = lax.psum(partial_sum, 'rep')]
    dynamic_slice x5 -> x0, local copies, waits for them, and re-layouts: 3.33 us -> none  [the longest x3 1.8 us: shards(): left_half = lax.dynamic_slice_in_dim(current, rep_index * half, half, 1)]
  transfers between devices with their start and end apart: 5 -> 0, of which waited for: 5 -> 0; matrix products, arithmetic and copies ran while one was open for 1% -> 0% of each run, Pallas kernels for 0% -> 0%
where the time goes in v1:
time: 74.7 us; the launch traced here: 74.4 us
  Pallas kernels  71 us (95%)
  local copies, waits for them, and re-layouts  3.42 us (5%)
    pallas_call x1, Pallas kernels, shards(): pl.pallas_call(kernel, out_shape=jax.ShapeDtypeStruct(density.shape, bf16...  71 us
    unnamed x7, local copies, waits for them, and re-layouts  3.42 us

profile of v1, /device:TPU:1, one launch (start us, length us, event | category | flops | bytes accessed | tf_op | source)
XLA Modules:
  0.0 74.4 jit_solution(18413851488654122857)
XLA Ops:
  0.0 0.0 copy-start
  0.0 1.1 %copy-done = bf16[768,384]{1,0:T(8,128)(2,1)S(1)} copy-done((bf16[768,384]{1,0:T(8,128)(2,1)S(1)}, bf16[768,384]{1,0:T(8,128)(2,1)}, u32[]{:S(2)}) %copy-start) | copy-done | bytes 589848
  1.1 0.0 copy-start.1
  1.1 0.8 %copy-done.1 = s32[2,48,48]{2,1,0:T(8,128)S(1)} copy-done((s32[2,48,48]{2,1,0:T(8,128)S(1)}, s32[2,48,48]{2,1,0:T(8,128)}, u32[]{:S(2)}) %copy-start.1) | copy-done | bytes 18456
  1.9 0.0 copy-start.2
  1.9 0.7 copy-done.2
  2.6 71.0 %purify.1 = bf16[768,384]{1,0:T(8,128)(2,1)S(1)} custom-call(s32[48,48]{1,0:T(8,128)S(1)} %copy-done.2, s32[2,48,48]{2,1,0:T(8,128)S(1)} %copy-done.1, bf16[768,384]{1,0:T(8,128)(2,1)S(1)} %copy-done), custom_call_target="tpu_custom_call" | custom-call | flops 3623878656 | bytes 1179648 | tf_op jit(solution)/shard_map/purify/pallas_call | solution.py:256
  73.6 0.8 %copy.5 = bf16[768,384]{1,0:T(8,128)(2,1)} copy(bf16[768,384]{1,0:T(8,128)(2,1)S(1)} %purify.1) | data formatting | bytes 1179648
Async XLA Ops:
  0.0 1.1 %copy-start = (bf16[768,384]{1,0:T(8,128)(2,1)S(1)}, bf16[768,384]{1,0:T(8,128)(2,1)}, u32[]{:S(2)}) copy-start(bf16[768,384]{1,0:T(8,128)(2,1)} %density.1) | copy-start | bytes 1769476
  1.1 0.8 %copy-start.1 = (s32[2,48,48]{2,1,0:T(8,128)S(1)}, s32[2,48,48]{2,1,0:T(8,128)}, u32[]{:S(2)}) copy-start(s32[2,48,48]{2,1,0:T(8,128)} %keep.1) | copy-start | bytes 55300
  1.9 0.7 copy-start.2

commit v2 on v1

--- a/solution.py
+++ b/solution.py
@@ -47,10 +47,12 @@
 QUEUES = queues()
 
 STAGES = [
-    (9, 5, 1, 0),
+    (8, 5, 1, 0),
+    (10, 5, 1, 1),
     (11, 6, 1, 1),
+    (12, 6, 2, 1),
     (13, 9, 2, 1),
-    (15, 11, 2, 2),
+    (14, 11, 2, 2),
     (16, 11, 3, 2),
     (17, 13, 3, 3),
     (18, 15, 4, 3),
@@ -58,7 +60,7 @@
 ]
 
 
-def kernel(pattern, keep, density, out, a0, a1, b0, b1, acc, own,
+def kernel(pattern_hbm, keep_hbm, density, out, a0, a1, b0, b1, acc, own, pattern, keep,
            recv_a, recv_b, recv_c, send, misc):
     z = lax.axis_index("row")
     col = lax.axis_index("col")
@@ -74,9 +76,24 @@
 
     load = pltpu.make_async_copy(density.at[half], own, misc.at[0])
     load.start()
+    load_pattern = pltpu.make_async_copy(pattern_hbm, pattern, misc.at[1])
+    load_pattern.start()
+    load_keep = pltpu.make_async_copy(keep_hbm, keep, misc.at[2])
+    load_keep.start()
     barrier = pltpu.get_barrier_semaphore()
     for target in targets + [other_core]:
         pl.semaphore_signal(barrier, inc=1, device_id=target, device_id_type=MESH)
+    slot_of = []
+    for dz in range(NZ):
+        for shared in range(2):
+            panel = ((z + dz) % NZ) * 2 + (1 - r if shared else r)
+            dx, dy = (panel // NY + NX - x) % NX, (panel % NY + NY - y) % NY
+            place = dx * NY + dy
+            slot = jnp.int32(0)
+            for j, (px, py) in enumerate(ORDER):
+                slot = jnp.where(place == px * NY + py, j, slot)
+            slot_of.append(slot)
+    load_pattern.wait()
     load.wait()
 
     def masked_store(mask, value, stores):
@@ -166,29 +183,37 @@
 
         def products(tiles, mine, shared, before):
             tiles0, mine0, shared0 = before
-
-            def body(i, carry):
-                dx, dy = jnp.int32(0), jnp.int32(0)
-                for j, place in enumerate(ORDER[:tiles]):
-                    if place != (0, 0):
-                        dx = jnp.where(i == j, place[0], dx)
-                        dy = jnp.where(i == j, place[1], dy)
+            items = []
+            for i in range(tiles0, tiles):
+                dx, dy = ORDER[i]
                 panel = ((x + dx) % NX) * NY + (y + dy) % NY
                 rp = panel % 2
                 dz = (panel // 2 + NZ - z) % NZ
                 far = jnp.where(dz > 4, NZ - dz, dz)
                 reach = jnp.where(rp == r, mine, shared)
-                reach0 = jnp.where(rp == r, mine0, shared0)
-                ready = jnp.where(far <= reach, 1, 0)
-                done = jnp.where((i < tiles0) & (far <= reach0), 1, 0)
-
-                @pl.when(ready > done)
+                items.append((jnp.int32(i), dz, rp, jnp.where(far <= reach, 1, 0)))
+            for reach0, reach, other in ((mine0, mine, 0), (shared0, shared, 1)):
+                for near in range(reach0 + 1, reach + 1):
+                    for dz in sorted({near, (NZ - near) % NZ}):
+                        slot = slot_of[dz * 2 + other]
+                        rp = 1 - r if other else r
+                        items.append((slot, jnp.int32(dz), rp, jnp.where(slot < tiles0, 1, 0)))
+
+            def body(n, carry):
+                slot, dz, rp, ready = items[0]
+                for m in range(1, len(items)):
+                    slot, dz, rp, ready = [
+                        jnp.where(n == m, new, old) for new, old in zip(items[m], (slot, dz, rp, ready))
+                    ]
+
+                @pl.when(ready > 0)
                 def _():
-                    acc[...] += jnp.dot(a[i], b[dz, rp], preferred_element_type=jnp.float32)
+                    acc[...] += jnp.dot(a[slot], b[dz, rp], preferred_element_type=jnp.float32)
 
                 return carry
 
-            lax.fori_loop(0, tiles, body, 0)
+            if items:
+                lax.fori_loop(0, len(items), body, 0)
 
         for k in range(4):
             issue(k)
@@ -217,46 +242,51 @@
                 for near in range(0, shared + 1):
                     for place in sorted({near, (NZ - near) % NZ}):
                         ensure_c(place)
-                if not stages:
+                products(tiles, mine, shared, before)
+                before = (tiles, mine, shared)
+                if len(stages) == 1:
                     for direction, queue in enumerate(QUEUES):
                         n = len(queue)
                         ref = a.at[pl.ds(0, n), pl.ds(0, CH)]
                         pltpu.make_async_copy(ref, ref, send.at[step, direction]).wait()
                     ref = b.at[:, 0]
                     pltpu.make_async_copy(ref, ref, send.at[step, 6]).wait()
-                products(tiles, mine, shared, before)
-                before = (tiles, mine, shared)
 
         if step == 0:
+            load_keep.wait()
             masked_store(
                 lambda i, j: keep[0, i, j], lambda rows, cols: acc[rows, cols],
                 [a1.at[0], b1.at[0, r]],
             )
-        else:
-            masked_store(
-                lambda i, j: keep[1, i, j],
-                lambda rows, cols: 2.0 * a[0, rows, cols].astype(jnp.float32) - acc[rows, cols],
-                [own],
-            )
-    remote = pltpu.make_async_remote_copy(
-        src_ref=own, dst_ref=out.at[half], send_sem=misc.at[1], recv_sem=misc.at[2],
-        device_id=other_core, device_id_type=MESH,
-    )
-    remote.start()
-    local = pltpu.make_async_copy(own, out.at[half], misc.at[0])
-    local.start()
-    local.wait()
-    remote.wait()
+
+    copies = []
+    for i in range(3):
+        rows = slice(i * BS, (i + 1) * BS)
+        for j in range(3):
+            cols = slice(j * BS, (j + 1) * BS)
+            block = 2.0 * a1[0, rows, cols].astype(jnp.float32) - acc[rows, cols]
+            kept = keep[1, z * 6 + r * 3 + i, col * 3 + j] > 0
+            own[rows, cols] = jnp.where(kept, block, jnp.zeros_like(block)).astype(jnp.bfloat16)
+        there = out.at[pl.ds(pl.multiple_of(r * H + i * BS, BS), BS)]
+        remote = pltpu.make_async_remote_copy(
+            src_ref=own.at[rows], dst_ref=there, send_sem=misc.at[3 + i], recv_sem=misc.at[6 + i],
+            device_id=other_core, device_id_type=MESH,
+        )
+        remote.start()
+        local = pltpu.make_async_copy(own.at[rows], there, misc.at[i])
+        local.start()
+        copies += [remote, local]
+    for copy in copies:
+        copy.wait()
 
 
 def shards(density, pattern, keep):
-    smem = pl.BlockSpec(memory_space=pltpu.SMEM)
     hbm = pl.BlockSpec(memory_space=pl.ANY)
     bf16 = jnp.bfloat16
     return pl.pallas_call(
         kernel,
         out_shape=jax.ShapeDtypeStruct(density.shape, bf16),
-        in_specs=[smem, smem, hbm],
+        in_specs=[hbm, hbm, hbm],
         out_specs=hbm,
         scratch_shapes=[
             pltpu.VMEM((16, H, H), bf16),
@@ -265,16 +295,18 @@
             pltpu.VMEM((NZ, 2, H, H), bf16),
             pltpu.VMEM((H, H), jnp.float32),
             pltpu.VMEM((H, H), bf16),
+            pltpu.SMEM(pattern.shape, jnp.int32),
+            pltpu.SMEM(keep.shape, jnp.int32),
             pltpu.SemaphoreType.DMA((2, 16, 4)),
             pltpu.SemaphoreType.DMA((2, NZ, 4)),
             pltpu.SemaphoreType.DMA((2, NZ)),
             pltpu.SemaphoreType.DMA((2, 7)),
-            pltpu.SemaphoreType.DMA((3,)),
+            pltpu.SemaphoreType.DMA((9,)),
         ],
         name="purify",
         cost_estimate=pl.CostEstimate(flops=2 * 2 * H * H * 6144, bytes_accessed=2 * 768 * H * 2, transcendentals=0),
         compiler_params=pltpu.CompilerParams(
-            collective_id=0, has_side_effects=True, vmem_limit_bytes=48 * 2**20
+            collective_id=0, has_side_effects=True, vmem_limit_bytes=60 * 2**20
         ),
     )(pattern, keep, density)
 

time: 74.7 us -> 69.6 us (0.932)
  Pallas kernels: 71 us -> 67.5 us
  local copies, waits for them, and re-layouts: 3.42 us -> 1.94 us
    pallas_call x1, Pallas kernels: 71 us -> 67.5 us  [shards(): pl.pallas_call(kernel, out_shape=jax.ShapeDtypeStruct(density.shape, bf16...]
    unnamed x7 -> x1, local copies, waits for them, and re-layouts: 3.42 us -> 1.94 us
where the time goes in v2:
time: 69.6 us; the launch traced here: 69.5 us
  Pallas kernels  67.5 us (97%)
  local copies, waits for them, and re-layouts  1.94 us (3%)
    pallas_call x1, Pallas kernels, shards(): pl.pallas_call(kernel, out_shape=jax.ShapeDtypeStruct(density.shape, bf16...  67.5 us
    unnamed x1, local copies, waits for them, and re-layouts  1.94 us

profile of v2, /device:TPU:1, one launch (start us, length us, event | category | flops | bytes accessed | tf_op | source)
XLA Modules:
  0.0 69.5 jit_solution(12785529511010670083)
XLA Ops:
  0.0 67.5 %purify.1 = bf16[768,384]{1,0:T(8,128)(2,1)} custom-call(s32[48,48]{1,0:T(8,128)} %pattern_hbm.1, s32[2,48,48]{2,1,0:T(8,128)} %keep_hbm.1, bf16[768,384]{1,0:T(8,128)(2,1)} %density.1), custom_call_target="tpu_custom_call" | custom-call | flops 3623878656 | bytes 1179648 | tf_op jit(solution)/shard_map/purify/pallas_call | solution.py:286
  67.5 1.9 %copy.5 = bf16[768,384]{1,0:T(8,128)(2,1)} copy(bf16[768,384]{1,0:T(8,128)(2,1)} %purify.1) | data formatting | bytes 1179648

commit v3 on v0

v3 whole, which is shorter than its diff:
```python
import jax
import jax.numpy as jnp
from jax import lax
from jax.experimental import pallas as pl
from jax.experimental.pallas import tpu as pltpu
from jax.sharding import PartitionSpec as P

BS = 128
NX, NY, NZ = 4, 4, 8
H = 384
CH = 96
HH = 192
Z_ROWS = (HH, CH)
WIDE = 256
FIRST_ROW = (0, 192, 96, 288)
COLS = (slice(0, WIDE), slice(WIDE, H))
GROUP = 2
MESH = pl.DeviceIdType.MESH

ORDER_UPPER = [
    (0, 0), (1, 0), (3, 0), (0, 1), (0, 3), (3, 3), (2, 0), (0, 2),
    (3, 2), (2, 3), (3, 1), (1, 3), (1, 1), (2, 2), (2, 1), (1, 2),
]
ORDER_REST = [
    (0, 0), (1, 0), (0, 1), (2, 0), (0, 2), (1, 1), (3, 0), (0, 3),
    (2, 1), (1, 2), (3, 2), (2, 3), (3, 1), (1, 3), (3, 3), (2, 2),
]
ORDER_LAST = [
    (0, 0), (1, 0), (3, 0), (0, 1), (0, 3), (3, 3), (3, 1), (1, 3),
    (1, 1), (2, 0), (0, 2), (3, 2), (2, 3), (1, 2), (2, 1), (2, 2),
]
ORDERS = [ORDER_UPPER, ORDER_REST, ORDER_LAST]

X_UP = [
    ((0, 0), 0), ((0, 0), 2), ((0, 0), 1), ((3, 0), 0), ((0, 3), 2), ((0, 1), 2), ((3, 0), 2), ((0, 2), 2),
    ((3, 3), 2), ((3, 1), 2), ((3, 2), 2), ((0, 0), 3), ((0, 2), 3), ((0, 1), 3), ((0, 3), 3),
]
X_DOWN = [
    ((0, 0), 0), ((0, 0), 2), ((0, 0), 1), ((0, 0), 3), ((1, 0), 1), ((0, 1), 3), ((0, 3), 3), ((1, 0), 3),
    ((0, 2), 3), ((0, 3), 2), ((0, 1), 2), ((0, 2), 2), ((1, 1), 3), ((1, 3), 3), ((1, 2), 3),
]
X_UP_LAST = [
    ((0, 0), 0), ((0, 0), 2), ((0, 0), 1), ((0, 0), 3), ((3, 0), 0), ((0, 3), 2), ((0, 3), 3), ((0, 1), 2),
    ((0, 1), 3), ((3, 0), 2), ((0, 2), 2), ((0, 2), 3), ((3, 3), 2), ((3, 1), 2), ((3, 2), 2),
]
X_DOWN_LAST = [
    ((0, 0), 0), ((0, 0), 2), ((0, 0), 1), ((0, 0), 3), ((1, 0), 1), ((0, 3), 3), ((0, 3), 2), ((0, 1), 3),
    ((0, 1), 2), ((1, 0), 3), ((0, 2), 3), ((0, 2), 2), ((1, 3), 3), ((1, 1), 3), ((1, 2), 3),
]


def swapped(queue):
    return [((dy, dx), (chunk + 2) % 4) for (dx, dy), chunk in queue]


Z_UP = [
    (0, 0, 0), (0, 0, 1), (0, 1, 0), (7, 0, 0), (7, 0, 1), (0, 1, 1), (6, 0, 0),
    (7, 1, 0), (6, 0, 1), (7, 1, 1), (6, 1, 0), (5, 0, 0), (6, 1, 1), (5, 1, 0),
]
Z_DOWN = [
    (0, 0, 0), (0, 0, 1), (0, 1, 1), (1, 0, 1), (1, 0, 0), (0, 1, 0), (2, 0, 1),
    (1, 1, 1), (2, 0, 0), (1, 1, 0), (2, 1, 1), (3, 0, 1), (2, 1, 0), (3, 1, 1),
]
Z_UP_LAST = [(dz, 0, chunk) for dz in (0, 7, 6) for chunk in range(4)] + [(5, 0, 0), (5, 0, 1)]
Z_DOWN_LAST = [(dz, 0, chunk) for dz in (0, 1, 2) for chunk in (3, 2, 1, 0)] + [(3, 0, 3), (3, 0, 2)]
QUEUES = [
    [X_UP, X_DOWN, swapped(X_UP), swapped(X_DOWN), Z_UP, Z_DOWN],
    [X_UP_LAST, X_DOWN_LAST, swapped(X_UP_LAST), swapped(X_DOWN_LAST), Z_UP_LAST, Z_DOWN_LAST],
]

STAGES = [
    [
        (8, 0, 5, 1, 1),
        (10, 0, 6, 2, 1),
        (10, 1, 3, 1, 0),
        (11, 0, 8, 2, 2),
        (13, 0, 12, 3, 2),
        (13, 1, 5, 2, 1),
        (15, 0, 14, 3, 3),
        (15, 1, 6, 2, 2),
        (15, 0, 16, 4, 3),
        (15, 1, 8, 2, 2),
        (15, 1, 10, 3, 2),
        (15, 0, 16, 4, 4),
        (15, 1, 14, 4, 3),
        (15, 1, 16, 4, 4),
    ],
    [
        (8, 2, 5, 1, 0),
        (10, 2, 5, 1, 1),
        (11, 2, 6, 1, 1),
        (12, 2, 6, 2, 1),
        (13, 2, 9, 2, 1),
        (14, 2, 11, 2, 2),
        (15, 2, 11, 3, 2),
        (15, 2, 13, 3, 3),
        (15, 2, 15, 4, 3),
        (15, 2, 16, 4, 4),
    ],
]


def kernel(pattern_hbm, keep_hbm, density, out, a0, a1, wide0, slim0, b1, acc, own, pattern, keep,
           recv_a, recv_b, recv_c, send, misc):
    z = lax.axis_index("row")
    col = lax.axis_index("col")
    r = lax.axis_index("rep")
    x, y = col // NY, col % NY

    def at(dx, dy, dz):
        return ((z + dz) % NZ, ((x + dx) % NX) * NY + (y + dy) % NY, r)

    targets = [at(1, 0, 0), at(3, 0, 0), at(0, 1, 0), at(0, 3, 0), at(0, 0, 1), at(0, 0, 7)]
    other_core = (z, col, 1 - r)

    barrier = pltpu.get_barrier_semaphore()
    for target in targets + [other_core]:
        pl.semaphore_signal(barrier, inc=1, device_id=target, device_id_type=MESH)
    load = pltpu.make_async_copy(density.at[pl.ds(pl.multiple_of(r * H, H), H)], own, misc.at[0])
    load.start()
    load_pattern = pltpu.make_async_copy(pattern_hbm, pattern, misc.at[1])
    load_pattern.start()
    load_keep = pltpu.make_async_copy(keep_hbm, keep, misc.at[2])
    load_keep.start()

    meets = []
    for dz in range(NZ):
        for other in range(2):
            panel = ((z + dz) % NZ) * 2 + (1 - r if other else r)
            place = ((panel // NY + NX - x) % NX) * NY + (panel % NY + NY - y) % NY
            ranks = []
            for order in ORDERS:
                rank = jnp.int32(0)
                for j, (px, py) in enumerate(order):
                    rank = jnp.where(place == px * NY + py, j, rank)
                ranks.append(rank)
            meets.append((place, ranks))
    load_pattern.wait()
    load.wait()

    def masked_store(mask, value, store, rows, cols):
        row = rows.start
        while row < rows.stop:
            row_end = min(rows.stop, (row // BS + 1) * BS)
            for j in range(cols.start // BS, cols.stop // BS):
                kept = mask(z * 6 + r * 3 + row // BS, col * 3 + j) > 0
                here, there = slice(row, row_end), slice(j * BS, (j + 1) * BS)
                block = value(here, there)
                store(here, there, jnp.where(kept, block, jnp.zeros_like(block)).astype(jnp.bfloat16))
            row = row_end

    def store_first(rows, cols, block):
        a0[0, rows, cols] = block
        if cols.start < WIDE:
            wide0[0, r, rows, cols] = block
        else:
            slim0[0, r, rows, slice(cols.start - WIDE, cols.stop - WIDE)] = block

    def store_second(rows, cols, block):
        a1[0, rows, cols] = block
        b1[0, r, rows, cols] = block

    def remote(src, dst, send_sem, recv_sem, target):
        pltpu.make_async_remote_copy(
            src_ref=src, dst_ref=dst, send_sem=send_sem, recv_sem=recv_sem,
            device_id=target, device_id_type=MESH,
        ).start()

    def arrived(ref, sem):
        pltpu.make_async_copy(ref, ref, sem).wait()

    def there_of(direction, place):
        if direction < 4:
            shift = ((3, 0), (1, 0), (0, 3), (0, 1))[direction]
            return ((place[0] + shift[0]) % NX, (place[1] + shift[1]) % NY)
        return (place + (7, 1)[direction - 4]) % NZ

    def slot_of(place):
        return place[0] * NY + place[1]

    def chunk_rows(chunk):
        return pl.ds(FIRST_ROW[chunk], CH)

    def send_chunk(step, a, direction, place, chunk, cols):
        there = there_of(direction, place)
        remote(
            a.at[slot_of(place), chunk_rows(chunk), cols], a.at[slot_of(there), chunk_rows(chunk), cols],
            send.at[step, direction], recv_a.at[step, slot_of(there), chunk], targets[direction],
        )

    def send_piece(step, b, direction, place, part, chunk, cols=None):
        there = there_of(direction, place)
        rows = pl.ds(chunk * Z_ROWS[step], Z_ROWS[step])
        src, dst = b.at[place, r, rows], b.at[there, r, rows]
        if cols is not None:
            src, dst = b.at[place, r, rows, cols], b.at[there, r, rows, cols]
        remote(src, dst, send.at[step, direction], recv_b.at[step, there, part, chunk], targets[direction])

    def send_early(step, a):
        for chunks, directions in (((0, 2), (0, 1)), ((2, 0), (2, 3))):
            for chunk in chunks:
                for direction in directions:
                    send_chunk(step, a, direction, (0, 0), chunk, pl.ds(0, WIDE))
        for direction in (4, 5):
            if step == 0:
                send_piece(step, wide0, direction, 0, 0, 0)
            else:
                for chunk in (0, 1):
                    send_piece(step, b1, direction, 0, 0, chunk, pl.ds(0, WIDE))

    upper, lower, full = slice(0, HH), slice(HH, H), slice(0, H)
    masked = lambda rows, cols: masked_store(
        lambda i, j: pattern[i, j], lambda i, j: own[i, j], store_first, rows, cols
    )
    masked(upper, COLS[0])
    pl.semaphore_wait(barrier, 7)
    send_early(0, a0)
    masked(upper, COLS[1])
    masked(lower, full)

    for step, (a, parts) in enumerate(((a0, (wide0, slim0)), (a1, (b1,)))):
        waited = set()

        def once(*key):
            if key in waited:
                return False
            waited.add(key)
            return True

        def ensure_a(place, chunk):
            if place != (0, 0) and once("a", place, chunk):
                arrived(a.at[slot_of(place), chunk_rows(chunk)], recv_a.at[step, slot_of(place), chunk])

        def ensure_b(place, part, chunk):
            if place != 0 and once("b", place, part, chunk):
                arrived(parts[part].at[place, r, pl.ds(chunk * Z_ROWS[step], Z_ROWS[step])], recv_b.at[step, place, part, chunk])

        def ensure_c(place, part):
            if once("c", place, part):
                arrived(parts[part].at[place, 1 - r], recv_c.at[step, place, part])

        def share(place, part):
            if once("s", place, part):
                ref = parts[part].at[place, r]
                remote(ref, ref, send.at[step, 6], recv_c.at[step, place, part], other_core)

        def issue(k):
            for direction, queue in enumerate(QUEUES[step]):
                if k >= len(queue):
                    continue
                rest = pl.ds(WIDE, H - WIDE)
                if direction < 4:
                    place, chunk = queue[k]
                    ensure_a(place, chunk)
                    early = place == (0, 0) and chunk in (0, 2)
                    send_chunk(step, a, direction, place, chunk, rest if early else pl.ds(0, H))
                else:
                    place, part, chunk = queue[k]
                    ensure_b(place, part, chunk)
                    if step == 1:
                        send_piece(step, b1, direction, place, 0, chunk, rest if place == 0 and chunk < 2 else None)
                    elif (place, part, chunk) != (0, 0, 0):
                        send_piece(step, parts[part], direction, place, part, chunk)
            for place in range(1, NZ):
                for part in range(len(parts)):
                    if all(("b", place, part, chunk) in waited for chunk in range(H // Z_ROWS[step])):
                        share(place, part)

        def products(region, count, mine, shared, before):
            count0, mine0, shared0 = before
            order = ORDERS[region]
            items = []
            for i in range(count0, count):
                dx, dy = order[i]
                panel = ((x + dx) % NX) * NY + (y + dy) % NY
                rp = panel % 2
                dz = (panel // 2 + NZ - z) % NZ
                far = jnp.where(dz > 4, NZ - dz, dz)
                reach = jnp.where(rp == r, mine, shared)
                items.append((jnp.int32(slot_of((dx, dy))), dz, rp, jnp.where(far <= reach, 1, 0)))
            for reach0, reach, other in ((mine0, mine, 0), (shared0, shared, 1)):
                for near in range(reach0 + 1, reach + 1):
                    for dz in sorted({near, (NZ - near) % NZ}):
                        place, ranks = meets[dz * 2 + other]
                        rp = 1 - r if other else r
                        items.append((place, jnp.int32(dz), rp, jnp.where(ranks[region] < count0, 1, 0)))

            if not items:
                return
            total, picks = jnp.int32(0), []
            for slot, dz, rp, ready in items:
                picks.append((jnp.where(ready > 0, total, -1), slot * 16 + dz * 2 + rp))
                total = total + ready

            def add(first, size):
                sums = {}
                for n in range(size):
                    code = jnp.int32(0)
                    for rank, item in picks:
                        code = jnp.where(rank == first + n, item, code)
                    slot, dz, rp = code // 16, code // 2 % NZ, code % 2
                    if region == 0:
                        terms = [(upper, COLS[0], wide0)]
                    elif region == 1:
                        terms = [(lower, COLS[0], wide0), (full, COLS[1], slim0)]
                    else:
                        terms = [(full, full, b1)]
                    for rows, cols, b in terms:
                        term = jnp.dot(a[slot, rows], b[dz, rp], preferred_element_type=jnp.float32)
                        key = (rows.start, rows.stop, cols.start, cols.stop)
                        sums[key] = sums[key] + term if key in sums else term
                for (r0, r1, c0, c1), term in sums.items():
                    acc[r0:r1, c0:c1] += term

            size = GROUP
            while size > len(items):
                size //= 2

            @pl.loop(0, total // size)
            def _(j):
                add(j * size, size)

            while size > 1:
                size //= 2

                @pl.when(total // size % 2 == 1)
                def _():
                    add(total // (2 * size) * (2 * size), size)

        issue(0)
        issue(1)
        for part in range(len(parts)):
            share(0, part)
        issue(2)
        acc[...] = jnp.zeros_like(acc)

        before = [(0, -1, -1)] * 3
        stages = list(STAGES[step])
        for k in range(3, 15):
            issue(k)
            while stages and stages[0][0] == k + 1:
                _, region, count, mine, shared = stages.pop(0)
                needed = range(1 if region == 0 else len(parts))
                for place in ORDERS[region][:count]:
                    for chunk in (0, 2) if region == 0 else (0, 1, 2, 3):
                        ensure_a(place, chunk)
                for near in range(0, mine + 1):
                    for dz in sorted({near, (NZ - near) % NZ}):
                        for part in needed:
                            for chunk in range(H // Z_ROWS[step]):
                                ensure_b(dz, part, chunk)
                            share(dz, part)
                for near in range(0, shared + 1):
                    for dz in sorted({near, (NZ - near) % NZ}):
                        for part in needed:
                            ensure_c(dz, part)
                if not stages:
                    for direction, queue in enumerate(QUEUES[step]):
                        arrived(a.at[pl.ds(0, len(queue)), pl.ds(0, CH)], send.at[step, direction])
                    arrived(a.at[pl.ds(0, NZ)], send.at[step, 6])
                products(region, count, mine, shared, before[region])
                before[region] = (count, mine, shared)
                if step == 0 and region == 0 and (count, mine, shared) == (16, 4, 4):
                    masked = lambda rows, cols: masked_store(
                        lambda i, j: keep[0, i, j], lambda i, j: acc[i, j], store_second, rows, cols
                    )
                    load_keep.wait()
                    masked(upper, COLS[0])
                    send_early(1, a1)

        if step == 0:
            masked(upper, COLS[1])
            masked(lower, full)

    copies = []
    for i in range(3):
        rows = slice(i * BS, (i + 1) * BS)
        there = pl.ds(pl.multiple_of(r * H + i * BS, BS), BS)
        for j in range(3):
            cols = slice(j * BS, (j + 1) * BS)
            block = 2.0 * a1[0, rows, cols].astype(jnp.float32) - acc[rows, cols]
            kept = keep[1, z * 6 + r * 3 + i, col * 3 + j] > 0
            out[there, cols] = jnp.where(kept, block, jnp.zeros_like(block)).astype(jnp.bfloat16)
        copy = pltpu.make_async_remote_copy(
            src_ref=out.at[there], dst_ref=out.at[there], send_sem=misc.at[3 + i], recv_sem=misc.at[6 + i],
            device_id=other_core, device_id_type=MESH,
        )
        copy.start()
        copies.append(copy)
    for copy in copies:
        copy.wait()


def shards(density, pattern, keep):
    hbm = pl.BlockSpec(memory_space=pl.ANY)
    bf16 = jnp.bfloat16
    return pl.pallas_call(
        kernel,
        out_shape=pltpu.VMEM(density.shape, bf16),
        in_specs=[hbm, hbm, hbm],
        out_specs=pl.BlockSpec(memory_space=pltpu.VMEM),
        scratch_shapes=[
            pltpu.VMEM((NX * NY, H, H), bf16),
            pltpu.VMEM((NX * NY, H, H), bf16),
            pltpu.VMEM((NZ, 2, H, WIDE), bf16),
            pltpu.VMEM((NZ, 2, H, H - WIDE), bf16),
            pltpu.VMEM((NZ, 2, H, H), bf16),
            pltpu.VMEM((H, H), jnp.float32),
            pltpu.VMEM((H, H), bf16),
            pltpu.SMEM(pattern.shape, jnp.int32),
            pltpu.SMEM(keep.shape, jnp.int32),
            pltpu.SemaphoreType.DMA((2, NX * NY, 4)),
            pltpu.SemaphoreType.DMA((2, NZ, 2, 4)),
            pltpu.SemaphoreType.DMA((2, NZ, 2)),
            pltpu.SemaphoreType.DMA((2, 7)),
            pltpu.SemaphoreType.DMA((9,)),
        ],
        name="purify",
        cost_estimate=pl.CostEstimate(flops=2 * 2 * H * H * 6144, bytes_accessed=2 * 768 * H * 2, transcendentals=0),
        compiler_params=pltpu.CompilerParams(
            collective_id=0, has_side_effects=True, vmem_limit_bytes=60 * 2**20
        ),
    )(pattern, keep, density)


def solution(mesh):
    in_specs = (P("row", "col"), P(), P())
    out_specs = P("row", "col")
    return jax.shard_map(shards, mesh=mesh, in_specs=in_specs, out_specs=out_specs, check_vma=False)
```

time: 277 us -> 67.2 us (0.24)
  waiting for transfers between devices: 235 us -> 0 us
  Pallas kernels: 0 us -> 66.3 us
  between operations: 13.2 us -> 0.01 us
  matrix products: 12 us -> 0 us
  blocking collectives: 7.08 us -> 0 us
  local copies, waits for them, and re-layouts: 6.62 us -> 0.82 us
  other arithmetic: 3.44 us -> 0 us
    all_gather x4 -> x0, waiting for transfers between devices: 204 us -> none  [the longest x2 126 us: shards(): lax.all_gather(left_half, 'col', axis=1, tiled=True)]
    pallas_call x0 -> x1, Pallas kernels: none -> 66.3 us  [shards(): pl.pallas_call(kernel, out_shape=pltpu.VMEM(density.shape, bf16), in_spec...]
    psum x1 -> x0, waiting for transfers between devices: 30.5 us -> none  [shards(): square = lax.psum(partial_sum, 'rep')]
    dot_general x2 -> x0, matrix products: 12 us -> none  [shards(): jnp.dot(lax.all_gather(left_half, 'col', axis=1, tiled=True), column_rows...]
    psum x1 -> x0, blocking collectives: 7.08 us -> none  [shards(): square = lax.psum(partial_sum, 'rep')]
    dynamic_slice x5 -> x0, local copies, waits for them, and re-layouts: 3.33 us -> none  [the longest x3 1.8 us: shards(): left_half = lax.dynamic_slice_in_dim(current, rep_index * half, half, 1)]
  transfers between devices with their start and end apart: 5 -> 0, of which waited for: 5 -> 0; matrix products, arithmetic and copies ran while one was open for 1% -> 0% of each run, Pallas kernels for 0% -> 0%
where the time goes in v3:
time: 67.2 us; the launch traced here: 67.1 us
  Pallas kernels  66.3 us (99%)
  local copies, waits for them, and re-layouts  0.82 us (1%)
    pallas_call x1, Pallas kernels, shards(): pl.pallas_call(kernel, out_shape=pltpu.VMEM(density.shape, bf16), in_spec...  66.3 us

profile of v3, /device:TPU:1, one launch (start us, length us, event | category | flops | bytes accessed | tf_op | source)
XLA Modules:
  0.0 67.1 jit_solution(10803975088792602899)
XLA Ops:
  0.0 66.3 %purify.1 = bf16[768,384]{1,0:T(8,128)(2,1)S(1)} custom-call(s32[48,48]{1,0:T(8,128)} %pattern_hbm.1, s32[2,48,48]{2,1,0:T(8,128)} %keep_hbm.1, bf16[768,384]{1,0:T(8,128)(2,1)} %density.1), custom_call_target="tpu_custom_call" | custom-call | flops 3623878656 | bytes 1179648 | tf_op jit(solution)/shard_map/purify/pallas_call | solution.py:397
  66.3 0.8 %copy.5 = bf16[768,384]{1,0:T(8,128)(2,1)} copy(bf16[768,384]{1,0:T(8,128)(2,1)S(1)} %purify.1) | data formatting | bytes 1179648

commit v4 on v3

--- a/solution.py
+++ b/solution.py
@@ -14,38 +14,38 @@
 WIDE = 256
 FIRST_ROW = (0, 192, 96, 288)
 COLS = (slice(0, WIDE), slice(WIDE, H))
-GROUP = 2
+GROUP = 4
 MESH = pl.DeviceIdType.MESH
 
 ORDER_UPPER = [
-    (0, 0), (1, 0), (3, 0), (0, 1), (0, 3), (3, 3), (2, 0), (0, 2),
-    (3, 2), (2, 3), (3, 1), (1, 3), (1, 1), (2, 2), (2, 1), (1, 2),
+    (0, 0), (1, 0), (3, 0), (0, 1), (0, 3), (3, 3), (1, 1), (3, 1),
+    (1, 3), (2, 0), (0, 2), (3, 2), (2, 3), (2, 1), (1, 2), (2, 2),
 ]
 ORDER_REST = [
-    (0, 0), (1, 0), (0, 1), (2, 0), (0, 2), (1, 1), (3, 0), (0, 3),
-    (2, 1), (1, 2), (3, 2), (2, 3), (3, 1), (1, 3), (3, 3), (2, 2),
+    (0, 0), (1, 0), (3, 0), (0, 1), (0, 3), (1, 1), (2, 0), (0, 2),
+    (2, 1), (1, 2), (3, 1), (1, 3), (2, 3), (3, 2), (2, 2), (3, 3),
 ]
 ORDER_LAST = [
-    (0, 0), (1, 0), (3, 0), (0, 1), (0, 3), (3, 3), (3, 1), (1, 3),
-    (1, 1), (2, 0), (0, 2), (3, 2), (2, 3), (1, 2), (2, 1), (2, 2),
+    (0, 0), (1, 0), (3, 0), (0, 1), (0, 3), (3, 3), (1, 3), (1, 1),
+    (3, 1), (2, 0), (0, 2), (2, 3), (3, 2), (2, 1), (1, 2), (2, 2),
 ]
 ORDERS = [ORDER_UPPER, ORDER_REST, ORDER_LAST]
 
 X_UP = [
-    ((0, 0), 0), ((0, 0), 2), ((0, 0), 1), ((3, 0), 0), ((0, 3), 2), ((0, 1), 2), ((3, 0), 2), ((0, 2), 2),
-    ((3, 3), 2), ((3, 1), 2), ((3, 2), 2), ((0, 0), 3), ((0, 2), 3), ((0, 1), 3), ((0, 3), 3),
+    ((0, 0), 0), ((0, 0), 2), ((0, 0), 1), ((0, 0), 3), ((3, 0), 0), ((0, 3), 2), ((0, 1), 2), ((3, 0), 2),
+    ((0, 2), 2), ((3, 3), 2), ((3, 1), 2), ((3, 2), 2), ((0, 1), 3), ((0, 2), 3), ((0, 3), 3),
 ]
 X_DOWN = [
-    ((0, 0), 0), ((0, 0), 2), ((0, 0), 1), ((0, 0), 3), ((1, 0), 1), ((0, 1), 3), ((0, 3), 3), ((1, 0), 3),
-    ((0, 2), 3), ((0, 3), 2), ((0, 1), 2), ((0, 2), 2), ((1, 1), 3), ((1, 3), 3), ((1, 2), 3),
+    ((0, 0), 0), ((0, 0), 2), ((0, 0), 1), ((0, 0), 3), ((0, 3), 2), ((0, 1), 2), ((1, 0), 1), ((0, 1), 3),
+    ((0, 3), 3), ((0, 2), 2), ((0, 2), 3), ((1, 0), 3), ((1, 1), 3), ((1, 3), 3), ((1, 2), 3),
 ]
 X_UP_LAST = [
-    ((0, 0), 0), ((0, 0), 2), ((0, 0), 1), ((0, 0), 3), ((3, 0), 0), ((0, 3), 2), ((0, 3), 3), ((0, 1), 2),
+    ((0, 0), 0), ((0, 0), 2), ((0, 0), 1), ((0, 0), 3), ((3, 0), 0), ((0, 3), 2), ((0, 1), 2), ((0, 3), 3),
     ((0, 1), 3), ((3, 0), 2), ((0, 2), 2), ((0, 2), 3), ((3, 3), 2), ((3, 1), 2), ((3, 2), 2),
 ]
 X_DOWN_LAST = [
-    ((0, 0), 0), ((0, 0), 2), ((0, 0), 1), ((0, 0), 3), ((1, 0), 1), ((0, 3), 3), ((0, 3), 2), ((0, 1), 3),
-    ((0, 1), 2), ((1, 0), 3), ((0, 2), 3), ((0, 2), 2), ((1, 3), 3), ((1, 1), 3), ((1, 2), 3),
+    ((0, 0), 0), ((0, 0), 2), ((0, 0), 1), ((0, 0), 3), ((0, 3), 2), ((0, 1), 2), ((1, 0), 1), ((0, 3), 3),
+    ((0, 1), 3), ((1, 0), 3), ((0, 2), 3), ((0, 2), 2), ((1, 3), 3), ((1, 1), 3), ((1, 2), 3),
 ]
 
 
@@ -54,15 +54,15 @@
 
 
 Z_UP = [
-    (0, 0, 0), (0, 0, 1), (0, 1, 0), (7, 0, 0), (7, 0, 1), (0, 1, 1), (6, 0, 0),
-    (7, 1, 0), (6, 0, 1), (7, 1, 1), (6, 1, 0), (5, 0, 0), (6, 1, 1), (5, 1, 0),
-]
-Z_DOWN = [
-    (0, 0, 0), (0, 0, 1), (0, 1, 1), (1, 0, 1), (1, 0, 0), (0, 1, 0), (2, 0, 1),
-    (1, 1, 1), (2, 0, 0), (1, 1, 0), (2, 1, 1), (3, 0, 1), (2, 1, 0), (3, 1, 1),
-]
+    (0, 0, 0), (0, 0, 1), (0, 1, 0), (0, 1, 1), (7, 0, 0), (7, 0, 1), (7, 1, 0),
+    (7, 1, 1), (6, 0, 0), (6, 0, 1), (6, 1, 0), (5, 0, 0), (6, 1, 1), (5, 1, 0),
+]
+Z_DOWN = [((NZ - dz) % NZ, part, 1 - chunk) for dz, part, chunk in Z_UP]
 Z_UP_LAST = [(dz, 0, chunk) for dz in (0, 7, 6) for chunk in range(4)] + [(5, 0, 0), (5, 0, 1)]
-Z_DOWN_LAST = [(dz, 0, chunk) for dz in (0, 1, 2) for chunk in (3, 2, 1, 0)] + [(3, 0, 3), (3, 0, 2)]
+Z_DOWN_LAST = [
+    (0, 0, 0), (0, 0, 1), (0, 0, 3), (0, 0, 2), (1, 0, 0), (1, 0, 3), (1, 0, 2),
+    (1, 0, 1), (2, 0, 3), (2, 0, 2), (2, 0, 0), (2, 0, 1), (3, 0, 3), (3, 0, 2),
+]
 QUEUES = [
     [X_UP, X_DOWN, swapped(X_UP), swapped(X_DOWN), Z_UP, Z_DOWN],
     [X_UP_LAST, X_DOWN_LAST, swapped(X_UP_LAST), swapped(X_DOWN_LAST), Z_UP_LAST, Z_DOWN_LAST],
@@ -70,27 +70,26 @@
 
 STAGES = [
     [
-        (8, 0, 5, 1, 1),
-        (10, 0, 6, 2, 1),
-        (10, 1, 3, 1, 0),
-        (11, 0, 8, 2, 2),
-        (13, 0, 12, 3, 2),
-        (13, 1, 5, 2, 1),
-        (15, 0, 14, 3, 3),
-        (15, 1, 6, 2, 2),
+        (9, 0, 5, 1, 1),
+        (10, 1, 5, 1, 1),
+        (11, 0, 9, 2, 1),
+        (12, 0, 11, 2, 2),
+        (13, 1, 6, 2, 2),
+        (14, 0, 13, 2, 2),
+        (15, 0, 15, 3, 2),
+        (15, 0, 16, 3, 3),
+        (15, 1, 8, 2, 2),
         (15, 0, 16, 4, 3),
-        (15, 1, 8, 2, 2),
-        (15, 1, 10, 3, 2),
+        (15, 1, 12, 2, 2),
         (15, 0, 16, 4, 4),
         (15, 1, 14, 4, 3),
         (15, 1, 16, 4, 4),
     ],
     [
-        (8, 2, 5, 1, 0),
+        (9, 2, 5, 1, 0),
         (10, 2, 5, 1, 1),
-        (11, 2, 6, 1, 1),
         (12, 2, 6, 2, 1),
-        (13, 2, 9, 2, 1),
+        (13, 2, 9, 2, 2),
         (14, 2, 11, 2, 2),
         (15, 2, 11, 3, 2),
         (15, 2, 13, 3, 3),
@@ -202,9 +201,9 @@
                 for direction in directions:
                     send_chunk(step, a, direction, (0, 0), chunk, pl.ds(0, WIDE))
         for direction in (4, 5):
-            if step == 0:
+            if step == 0 and direction == 4:
                 send_piece(step, wide0, direction, 0, 0, 0)
-            else:
+            elif step == 1:
                 for chunk in (0, 1):
                     send_piece(step, b1, direction, 0, 0, chunk, pl.ds(0, WIDE))
 
@@ -259,7 +258,7 @@
                     ensure_b(place, part, chunk)
                     if step == 1:
                         send_piece(step, b1, direction, place, 0, chunk, rest if place == 0 and chunk < 2 else None)
-                    elif (place, part, chunk) != (0, 0, 0):
+                    elif (direction, place, part, chunk) != (4, 0, 0, 0):
                         send_piece(step, parts[part], direction, place, part, chunk)
             for place in range(1, NZ):
                 for part in range(len(parts)):
@@ -293,24 +292,23 @@
                 total = total + ready
 
             def add(first, size):
-                sums = {}
+                slots, halves = [], []
                 for n in range(size):
                     code = jnp.int32(0)
                     for rank, item in picks:
                         code = jnp.where(rank == first + n, item, code)
-                    slot, dz, rp = code // 16, code // 2 % NZ, code % 2
-                    if region == 0:
-                        terms = [(upper, COLS[0], wide0)]
-                    elif region == 1:
-                        terms = [(lower, COLS[0], wide0), (full, COLS[1], slim0)]
-                    else:
-                        terms = [(full, full, b1)]
-                    for rows, cols, b in terms:
-                        term = jnp.dot(a[slot, rows], b[dz, rp], preferred_element_type=jnp.float32)
-                        key = (rows.start, rows.stop, cols.start, cols.stop)
-                        sums[key] = sums[key] + term if key in sums else term
-                for (r0, r1, c0, c1), term in sums.items():
-                    acc[r0:r1, c0:c1] += term
+                    slots.append(lax.div(code, 16))
+                    halves.append((lax.rem(lax.div(code, 2), NZ), lax.rem(code, 2)))
+                if region == 0:
+                    terms = [(upper, COLS[0], wide0)]
+                elif region == 1:
+                    terms = [(lower, COLS[0], wide0), (full, COLS[1], slim0)]
+                else:
+                    terms = [(full, full, b1)]
+                for rows, cols, b in terms:
+                    left = jnp.concatenate([a[slot, rows] for slot in slots], axis=1)
+                    right = jnp.concatenate([b[dz, rp] for dz, rp in halves], axis=0)
+                    acc[rows, cols] += jnp.dot(left, right, preferred_element_type=jnp.float32)
 
             size = GROUP
             while size > len(items):

time: 67.2 us -> 67 us (level)
  no operation moved by 1% of the time
where the time goes in v4:
time: 67 us; the launch traced here: 66.9 us
  Pallas kernels  66.1 us (99%)
  local copies, waits for them, and re-layouts  0.82 us (1%)
    pallas_call x1, Pallas kernels, shards(): pl.pallas_call(kernel, out_shape=pltpu.VMEM(density.shape, bf16), in_spec...  66.1 us

profile of v4, /device:TPU:1, one launch (start us, length us, event | category | flops | bytes accessed | tf_op | source)
XLA Modules:
  0.0 66.9 jit_solution(10670533108698942307)
XLA Ops:
  0.0 66.1 %purify.1 = bf16[768,384]{1,0:T(8,128)(2,1)S(1)} custom-call(s32[48,48]{1,0:T(8,128)} %pattern_hbm.1, s32[2,48,48]{2,1,0:T(8,128)} %keep_hbm.1, bf16[768,384]{1,0:T(8,128)(2,1)} %density.1), custom_call_target="tpu_custom_call" | custom-call | flops 3623878656 | bytes 1179648 | tf_op jit(solution)/shard_map/purify/pallas_call | solution.py:395
  66.1 0.8 %copy.5 = bf16[768,384]{1,0:T(8,128)(2,1)} copy(bf16[768,384]{1,0:T(8,128)(2,1)S(1)} %purify.1) | data formatting | bytes 1179648

commit v5 on v4

--- a/solution.py
+++ b/solution.py
@@ -70,12 +70,9 @@
 
 STAGES = [
     [
-        (9, 0, 5, 1, 1),
-        (10, 1, 5, 1, 1),
-        (11, 0, 9, 2, 1),
+        (10, 0, 7, 1, 1),
         (12, 0, 11, 2, 2),
         (13, 1, 6, 2, 2),
-        (14, 0, 13, 2, 2),
         (15, 0, 15, 3, 2),
         (15, 0, 16, 3, 3),
         (15, 1, 8, 2, 2),
@@ -86,11 +83,9 @@
         (15, 1, 16, 4, 4),
     ],
     [
-        (9, 2, 5, 1, 0),
         (10, 2, 5, 1, 1),
         (12, 2, 6, 2, 1),
         (13, 2, 9, 2, 2),
-        (14, 2, 11, 2, 2),
         (15, 2, 11, 3, 2),
         (15, 2, 13, 3, 3),
         (15, 2, 15, 4, 3),

time: 67 us -> 67 us (level)
  no operation moved by 1% of the time
where the time goes in v5:
time: 67 us; the launch traced here: 66.9 us
  Pallas kernels  66.1 us (99%)
  local copies, waits for them, and re-layouts  0.82 us (1%)
    pallas_call x1, Pallas kernels, shards(): pl.pallas_call(kernel, out_shape=pltpu.VMEM(density.shape, bf16), in_spec...  66.1 us

profile of v5, /device:TPU:1, one launch (start us, length us, event | category | flops | bytes accessed | tf_op | source)
XLA Modules:
  0.0 66.9 jit_solution(10191498985833972302)
XLA Ops:
  0.0 66.1 %purify.1 = bf16[768,384]{1,0:T(8,128)(2,1)S(1)} custom-call(s32[48,48]{1,0:T(8,128)} %pattern_hbm.1, s32[2,48,48]{2,1,0:T(8,128)} %keep_hbm.1, bf16[768,384]{1,0:T(8,128)(2,1)} %density.1), custom_call_target="tpu_custom_call" | custom-call | flops 3623878656 | bytes 1179648 | tf_op jit(solution)/shard_map/purify/pallas_call | solution.py:390
  66.1 0.8 %copy.5 = bf16[768,384]{1,0:T(8,128)(2,1)} copy(bf16[768,384]{1,0:T(8,128)(2,1)S(1)} %purify.1) | data formatting | bytes 1179648

commit v6 on v5

--- a/solution.py
+++ b/solution.py
@@ -77,8 +77,8 @@
         (15, 0, 16, 3, 3),
         (15, 1, 8, 2, 2),
         (15, 0, 16, 4, 3),
-        (15, 1, 12, 2, 2),
         (15, 0, 16, 4, 4),
+        (15, 1, 12, 3, 2),
         (15, 1, 14, 4, 3),
         (15, 1, 16, 4, 4),
     ],
@@ -227,7 +227,9 @@
 
         def ensure_b(place, part, chunk):
             if place != 0 and once("b", place, part, chunk):
-                arrived(parts[part].at[place, r, pl.ds(chunk * Z_ROWS[step], Z_ROWS[step])], recv_b.at[step, place, part, chunk])
+                ref = parts[part].at[place, r, pl.ds(chunk * Z_ROWS[step], Z_ROWS[step])]
+                arrived(ref, recv_b.at[step, place, part, chunk])
+                remote(ref, ref, send.at[step, 6], recv_c.at[step, place, part], other_core)
 
         def ensure_c(place, part):
             if once("c", place, part):
@@ -255,10 +257,6 @@
                         send_piece(step, b1, direction, place, 0, chunk, rest if place == 0 and chunk < 2 else None)
                     elif (direction, place, part, chunk) != (4, 0, 0, 0):
                         send_piece(step, parts[part], direction, place, part, chunk)
-            for place in range(1, NZ):
-                for part in range(len(parts)):
-                    if all(("b", place, part, chunk) in waited for chunk in range(H // Z_ROWS[step])):
-                        share(place, part)
 
         def products(region, count, mine, shared, before):
             count0, mine0, shared0 = before
@@ -342,7 +340,6 @@
                         for part in needed:
                             for chunk in range(H // Z_ROWS[step]):
                                 ensure_b(dz, part, chunk)
-                            share(dz, part)
                 for near in range(0, shared + 1):
                     for dz in sorted({near, (NZ - near) % NZ}):
                         for part in needed:

time: 67 us -> 66.7 us (level)
  no operation moved by 1% of the time
where the time goes in v6:
time: 66.7 us; the launch traced here: 66.6 us
  Pallas kernels  65.8 us (99%)
  local copies, waits for them, and re-layouts  0.82 us (1%)
    pallas_call x1, Pallas kernels, shards(): pl.pallas_call(kernel, out_shape=pltpu.VMEM(density.shape, bf16), in_spec...  65.8 us

profile of v6, /device:TPU:1, one launch (start us, length us, event | category | flops | bytes accessed | tf_op | source)
XLA Modules:
  0.0 66.6 jit_solution(9488607842713740063)
XLA Ops:
  0.0 65.8 %purify.1 = bf16[768,384]{1,0:T(8,128)(2,1)S(1)} custom-call(s32[48,48]{1,0:T(8,128)} %pattern_hbm.1, s32[2,48,48]{2,1,0:T(8,128)} %keep_hbm.1, bf16[768,384]{1,0:T(8,128)(2,1)} %density.1), custom_call_target="tpu_custom_call" | custom-call | flops 3623878656 | bytes 1179648 | tf_op jit(solution)/shard_map/purify/pallas_call | solution.py:387
  65.8 0.8 %copy.5 = bf16[768,384]{1,0:T(8,128)(2,1)} copy(bf16[768,384]{1,0:T(8,128)(2,1)S(1)} %purify.1) | data formatting | bytes 1179648

commit v7 on v6

--- a/solution.py
+++ b/solution.py
@@ -241,7 +241,8 @@
                 remote(ref, ref, send.at[step, 6], recv_c.at[step, place, part], other_core)
 
         def issue(k):
-            for direction, queue in enumerate(QUEUES[step]):
+            for direction in (4, 5, 0, 1, 2, 3):
+                queue = QUEUES[step][direction]
                 if k >= len(queue):
                     continue
                 rest = pl.ds(WIDE, H - WIDE)

time: 66.7 us -> 66.7 us (level)
  no operation moved by 1% of the time
where the time goes in v7:
time: 66.7 us; the launch traced here: 66.6 us
  Pallas kernels  65.8 us (99%)
  local copies, waits for them, and re-layouts  0.82 us (1%)
    pallas_call x1, Pallas kernels, shards(): pl.pallas_call(kernel, out_shape=pltpu.VMEM(density.shape, bf16), in_spec...  65.8 us

profile of v7, /device:TPU:1, one launch (start us, length us, event | category | flops | bytes accessed | tf_op | source)
XLA Modules:
  0.0 66.6 jit_solution(2432098166769656185)
XLA Ops:
  0.0 65.8 %purify.1 = bf16[768,384]{1,0:T(8,128)(2,1)S(1)} custom-call(s32[48,48]{1,0:T(8,128)} %pattern_hbm.1, s32[2,48,48]{2,1,0:T(8,128)} %keep_hbm.1, bf16[768,384]{1,0:T(8,128)(2,1)} %density.1), custom_call_target="tpu_custom_call" | custom-call | flops 3623878656 | bytes 1179648 | tf_op jit(solution)/shard_map/purify/pallas_call | solution.py:388
  65.8 0.8 %copy.5 = bf16[768,384]{1,0:T(8,128)(2,1)} copy(bf16[768,384]{1,0:T(8,128)(2,1)S(1)} %purify.1) | data formatting | bytes 1179648
